TPU v7x, 32 devices: a whole 2x2x4 slice. The times are simulated.
32 devices in a mesh: groups: 2 (over y), gx: 4 (over z), gy: 2 (over x), gz: 2 (over core).
Axes of the slice: x: 2, y: 2, z: 4, core: 2. Of those that a mesh axis runs over, the one named last changes fastest.
Arguments:
- field: bfloat16 [16, 8, 1024, 512], P('gz', ('groups', 'gx'), 'gy'), parts along dimension 1, may hold values from -6 to 6
- spectral: bfloat16 [1, 32, 32, 16, 1024], P(None, 'gx', 'gy', None, 'gz'), may hold values from -1.5 to 1.5
- pointwise: bfloat16 [1, 16, 16], replicated, may hold values from -1.5 to 1.5
- shift: float32 [1, 16], replicated, may hold values from -3 to 3
Outputs:
- result: bfloat16 [16, 8, 1024, 512], P('gz', ('groups', 'gx'), 'gy'), parts along dimension 1
There are 2 independent parts, one for each index of `groups`. A program takes and returns all parts, laid end to end along the dimension named above; an argument that names none is the same for every part. Nothing has to cross between parts.
All inputs are finite; a program needn't handle non-finite values.
Results may differ from a plain program's by a relative error of at most 0.0069.
Values may be sent and summed in bfloat16 or wider, within the bound.
A program may use at most 128 MiB of HBM per device.

v0:
```python
import math

import jax
import jax.numpy as jnp
from jax import lax
from jax.sharding import PartitionSpec as P

CH = 16
KX = 32
KY = 32
KZ = 32


def forward_phases(xs, ys, nx, ny):
    index = jnp.arange(KX * KY * 2, dtype=jnp.int32)
    mode = index // 2
    parity = index % 2
    kx = mode // KY - KX // 2
    ky = mode % KY - KY // 2
    phase = jnp.mod(
        kx[None, None, :] * xs[:, None, None] * ny + ky[None, None, :] * ys[None, :, None] * nx,
        nx * ny,
    )
    angle = phase.astype(jnp.float32) * (2.0 * math.pi / (nx * ny))
    return jnp.where(parity[None, None, :] == 0, jnp.cos(angle), jnp.sin(angle)).astype(
        jnp.bfloat16
    )


def inverse_phases(xs, ys, nx, ny):
    nrows = ys.shape[0]
    mode = jnp.arange(KX * KY, dtype=jnp.int32)
    kx = mode // KY - KX // 2
    ky = mode % KY - KY // 2
    column = jnp.arange(xs.shape[0] * nrows * 2, dtype=jnp.int32)
    parity = column % 2
    cell = column // 2
    xpos = jnp.take(xs, cell // nrows)
    ypos = jnp.take(ys, cell % nrows)
    phase = jnp.mod(kx[:, None] * xpos[None, :] * ny + ky[:, None] * ypos[None, :] * nx, nx * ny)
    angle = phase.astype(jnp.float32) * (2.0 * math.pi / (nx * ny))
    return jnp.where(parity[None, :] == 0, jnp.cos(angle), jnp.sin(angle)).astype(jnp.bfloat16)


def z_tables(zlen, kcount):
    cells = jnp.arange(zlen, dtype=jnp.int32)
    modes = jnp.arange(kcount, dtype=jnp.int32)
    angle = jnp.mod(cells[:, None] * modes[None, :], zlen).astype(jnp.float32) * (
        2.0 * math.pi / zlen
    )
    forward = jnp.concatenate([jnp.cos(angle), -jnp.sin(angle)], axis=1)
    weight = jnp.where(modes == 0, 1.0, 2.0).astype(jnp.float32)
    inverse = (forward * jnp.concatenate([weight, weight])[None, :]).T
    return (forward.astype(jnp.bfloat16), inverse.astype(jnp.bfloat16))


def split_flat(prod, channels, kcount):
    shaped = prod.reshape(channels, 2, kcount, KX * KY * 2)
    real = shaped[:, 0, :, 0::2] + shaped[:, 1, :, 1::2]
    imag = shaped[:, 1, :, 0::2] - shaped[:, 0, :, 1::2]
    return jnp.stack([real, imag], axis=1).reshape(channels, 2, kcount, KX, KY)


def join_flat(prod, channels, kcount, planes, nrows):
    shaped = prod.reshape(channels, 2, kcount, planes * nrows * 2)
    real = shaped[:, 0, :, 0::2] - shaped[:, 1, :, 1::2]
    imag = shaped[:, 0, :, 1::2] + shaped[:, 1, :, 0::2]
    joined = jnp.stack([real, imag], axis=1).transpose(0, 3, 1, 2)
    return joined.reshape(channels, planes, nrows, 2, kcount).astype(jnp.bfloat16)


def mix_modes(spec, weights):
    shaped = weights.reshape(weights.shape[0], weights.shape[1], CH, -1, 2, KY)
    w_real = shaped[:, :, :, :, 0]
    w_imag = shaped[:, :, :, :, 1]
    s_real = spec[:, :, :, 0]
    s_imag = spec[:, :, :, 1]
    m_real = jnp.einsum(
        "abiok,abik->abok", w_real, s_real, preferred_element_type=jnp.float32
    ) - jnp.einsum("abiok,abik->abok", w_imag, s_imag, preferred_element_type=jnp.float32)
    m_imag = jnp.einsum(
        "abiok,abik->abok", w_real, s_imag, preferred_element_type=jnp.float32
    ) + jnp.einsum("abiok,abik->abok", w_imag, s_real, preferred_element_type=jnp.float32)
    return jnp.stack([m_real, m_imag], axis=3).astype(jnp.bfloat16)


def on_device(field, spectral, pointwise, shift):
    count_x = lax.axis_size("gx")
    count_y = lax.axis_size("gy")
    split_z = 1
    channels, planes, rows, zlen = field.shape
    total_x = planes * count_x
    total_y = rows * count_y * split_z
    kx_each = KX // count_x
    kz_each = KZ // count_y
    x_here = lax.axis_index("gx") * planes + jnp.arange(planes, dtype=jnp.int32)
    y_here = lax.axis_index("gy") * split_z * rows + jnp.arange(rows, dtype=jnp.int32)
    start = lax.axis_index("gz") * channels
    fz, gz = z_tables(zlen, KZ)
    forward_scale = 1.0 / math.sqrt(total_x * total_y * zlen)
    inverse_scale = 1.0 / math.sqrt(2 * KX * KY * KZ)
    table = forward_phases(x_here, y_here, total_x, total_y)
    back = inverse_phases(x_here, y_here, total_x, total_y)
    everyone = lax.all_gather(field, "gz", axis=0, tiled=True)
    mixing_rows = lax.dynamic_slice_in_dim(pointwise[0], start, channels, 0)
    offsets = lax.dynamic_slice_in_dim(shift[0], start, channels, 0)
    zhat = jnp.dot(field.reshape(-1, zlen), fz, preferred_element_type=jnp.float32).astype(
        jnp.bfloat16
    )
    prod = lax.dot_general(
        zhat.reshape(channels, planes, rows, 2 * KZ),
        table,
        (((1, 2), (0, 1)), ((), ())),
        preferred_element_type=jnp.float32,
    )
    parts = split_flat(prod, channels, KZ)
    blocks = (
        parts.reshape(channels, 2, count_y, kz_each, count_x, kx_each, KY)
        .transpose(4, 2, 5, 3, 0, 1, 6)
        .reshape(count_x * count_y, kx_each, kz_each, channels, 2, KY)
    )
    owned = lax.psum_scatter(blocks, ("gx", "gy"), scatter_dimension=0, tiled=True)[0]
    spec = (owned * forward_scale).astype(jnp.bfloat16)
    inputs = lax.all_gather(spec, "gz", axis=2, tiled=True)
    mixed = mix_modes(inputs, spectral[0])
    every = lax.all_gather(mixed[None], ("gx", "gy"), axis=0, tiled=True)
    flat = (
        every.reshape(count_x, count_y, kx_each, kz_each, channels, 2, KY)
        .transpose(4, 5, 1, 3, 0, 2, 6)
        .reshape(channels * 2 * KZ, KX * KY)
    )
    prod = jnp.dot(flat, back, preferred_element_type=jnp.float32)
    lines = join_flat(prod, channels, KZ, planes, rows)
    spectral_out = (
        jnp.dot(lines.reshape(-1, 2 * KZ), gz, preferred_element_type=jnp.float32).reshape(
            channels, planes, rows, zlen
        )
        * inverse_scale
    )
    local = jnp.einsum("oi,ixyz->oxyz", mixing_rows, everyone, preferred_element_type=jnp.float32)
    field = jax.nn.gelu(spectral_out + local + offsets[:, None, None, None]).astype(jnp.bfloat16)
    return field


def solution(mesh):
    return jax.shard_map(
        on_device,
        mesh=mesh,
        in_specs=(P("gz", ("groups", "gx"), "gy", None), P(None, "gx", "gy", None, "gz"), P(), P()),
        out_specs=P("gz", ("groups", "gx"), "gy", None),
        check_vma=False,
    )
```

profile of v0, /device:TPU:0, one launch (start us, length us, event | category | flops | bytes accessed | tf_op | source)
XLA Modules:
  0.0 566.5 jit_solution(15652539664403566057)
XLA Ops:
  6.5 0.3 sine_negate_fusion
  6.8 3.6 convolution_convert_fusion
  10.4 0.2 copy.64
  10.6 0.2 copy.23
  10.8 19.2 %fusion.23 = f32[8,2,32,2048]{3,2,1,0:T(8,128)} fusion(bf16[8,2,32,512]{3,2,1,0:T(8,128)(2,1)S(1)} %bitcast.100, s32[512]{0:T(512)S(1)} %iota_add_fusion, s32[2048]{0:T(1024)S(1)} %get-tuple-element.18, s32[2048]{0:T(1024)S(1)} %get-tuple-element.17, pred[2048]{0:T(1024)(128)(4,1)S(1)} %fusion.64), kind=kOutput, calls=%fused_computation.40 | convolution fusion | flops 1092616192 | bytes 4739072 | tf_op jit(solution)/shard_map/dot_general | solution.py:110
  30.0 36.6 %slice.36 = f32[8,1,32,1024]{3,2,1,0:T(8,128)} slice(f32[8,2,32,2048]{3,2,1,0:T(8,128)} %fusion.23), slice={[0:8:1], [0:1:1], [0:32:1], [0:2048:2]} | slice | bytes 2097152 | tf_op jit(solution)/shard_map/slice | solution.py:59
  66.6 36.4 %slice.37 = f32[8,1,32,1024]{3,2,1,0:T(8,128)} slice(f32[8,2,32,2048]{3,2,1,0:T(8,128)} %fusion.23), slice={[0:8:1], [1:2:1], [0:32:1], [1:2048:2]} | slice | bytes 2097152 | tf_op jit(solution)/shard_map/slice | solution.py:59
  103.0 35.9 %slice.38 = f32[8,1,32,1024]{3,2,1,0:T(8,128)S(1)} slice(f32[8,2,32,2048]{3,2,1,0:T(8,128)} %fusion.23), slice={[0:8:1], [1:2:1], [0:32:1], [0:2048:2]} | slice | bytes 2097152 | tf_op jit(solution)/shard_map/slice | solution.py:60
  138.9 36.3 %slice.39 = f32[8,1,32,1024]{3,2,1,0:T(8,128)S(1)} slice(f32[8,2,32,2048]{3,2,1,0:T(8,128)} %fusion.23), slice={[0:8:1], [0:1:1], [0:32:1], [1:2048:2]} | slice | bytes 2097152 | tf_op jit(solution)/shard_map/slice | solution.py:60
  175.2 1.7 add.256
  176.9 2.7 stack.24
  179.6 6.5 %copy.24 = f32[8,1,2,16,4,8,32]{6,0,1,3,5,2,4:T(8,128)} copy(f32[8,1,2,16,4,8,32]{6,5,4,3,2,0,1:T(8,128)} %stack.24) | data formatting | bytes 2097152 | tf_op jit(solution)/shard_map/stack | solution.py:61
  186.2 0.2 sub.60
  186.4 2.7 stack.25
  189.1 4.8 copy.25
  193.9 4.1 pad_maximum_fusion
  198.0 0.0 reduce-scatter.2.cloned.1.call-update
  198.0 0.0 all-gather.4.cloned.1.call-start
  198.1 1.5 copy-done.2
  199.6 7.1 %reshape_squeeze.3 = bf16[8,16,16,8,2,32]{5,4,3,2,1,0:T(2,128)(2,1)} reshape(bf16[1,8,16,16,512]{4,3,2,1,0:T(8,128)(2,1)S(1)} %copy-done.2) | data formatting | bytes 4194304 | tf_op jit(solution)/shard_map/reshape;squeeze | solution.py:73
  206.7 20.2 %fusion.113 = (bf16[8,16,16,8,1,32]{5,4,3,2,1,0:T(2,128)(2,1)}, bf16[8,16,16,8,1,32]{5,4,3,2,1,0:T(2,128)(2,1)}) fusion(bf16[8,16,16,8,2,32]{5,4,3,2,1,0:T(2,128)(2,1)} %reshape_squeeze.3), kind=kLoop, calls=%fused_computation.180 | loop fusion | bytes 4194304 | tf_op jit(solution)/shard_map/slice | solution.py:75
  226.9 123.0 %reduce-scatter.2.cloned.1.call-done = f32[1,8,16,8,2,32]{5,3,4,2,1,0:T(8,128)} async-done(((f32[8,8,16,8,2,32]{5,3,4,2,1,0:T(8,128)}), f32[1,8,16,8,2,32]{5,3,4,2,1,0:T(8,128)}) %reduce-scatter.2.cloned.1.call-update) | async-done | bytes 262160 | tf_op jit(solution)/shard_map/reduce_scatter | solution.py:122
  349.9 1.3 multiply_convert_fusion
  351.2 2.6 all-gather
  353.8 0.2 fusion.48
  354.0 13.8 %fusion = (f32[8,16,32,8]{2,3,1,0:T(8,128)S(1)}, f32[8,16,32,8]{2,3,1,0:T(8,128)S(1)}, f32[8,16,32,8]{2,3,1,0:T(8,128)S(1)}, f32[8,16,32,8]{2,3,1,0:T(8,128)S(1)}) fusion(f32[8,16,32,16]{2,3,1,0:T(8,128)S(1)} %get-tuple-element.14, bf16[8,16,16,8,1,32]{5,4,3,2,1,0:T(2,128)(2,1)} %get-tuple-element.12, f32[8,16,32,16]{2,3,1,0:T(8,128)S(1)} %get-tuple-element.13, ...), kind=kLoop, calls=%fused_computation.6 | loop fusion | flops 5111808 | bytes 3145728 | tf_op jit(solution)/shard_map/abiok,abik->abok/dot_general | solution.py:78
  367.8 0.1 fusion.50
  367.9 0.1 fusion.51
  368.0 0.9 pad_maximum_fusion.1
  368.9 0.0 all-gather.6.cloned.1.call-start
  369.0 6.5 %copy.27 = bf16[8,1,512,512]{3,0,2,1:T(8,128)(2,1)} copy(bf16[8,1,512,512]{3,2,1,0:T(8,128)(2,1)} %param.4) | data formatting | bytes 8388608 | tf_op args[0]
  375.6 6.9 %gather_fusion = s32[1024]{0:T(1024)S(1)} fusion(s32[512]{0:T(512)S(1)} %iota_add_fusion, s32[1024]{0:T(1024)S(1)} %broadcast_clamp_fusion), kind=kCustom, calls=%fused_computation | custom fusion | bytes 12288 | tf_op jit(solution)/shard_map/jit(_take)/gather | solution.py:39
  382.5 0.1 pad_maximum_fusion.4
  382.5 0.1 dynamic-slice_bitcast_fusion
  382.6 58.8 %all-gather.4.cloned.1.call-done = bf16[8,8,16,8,2,32]{5,3,4,2,1,0:T(8,128)(2,1)} async-done(((bf16[1,8,16,8,2,32]{5,3,4,2,1,0:T(8,128)(2,1)}), bf16[8,8,16,8,2,32]{5,3,4,2,1,0:T(8,128)(2,1)}) %all-gather.4.cloned.1.call-update) | async-done | bytes 1048592 | tf_op jit(solution)/shard_map/all_gather | solution.py:126
  441.5 7.0 %copy.26 = bf16[8,2,2,16,4,8,32]{6,5,4,3,2,1,0:T(8,128)(2,1)} copy(bf16[8,2,2,16,4,8,32]{6,0,1,3,5,2,4:T(8,128)(2,1)} %bitcast.97) | data formatting | bytes 2097152 | tf_op jit(solution)/shard_map/transpose | solution.py:129
  448.5 7.1 %dot_general.43 = bf16[8,2,32,1024]{3,2,1,0:T(8,128)(2,1)S(1)} reshape(bf16[8,2,2,16,4,8,32]{6,5,4,3,2,1,0:T(8,128)(2,1)} %copy.26) | data formatting | bytes 2097152 | tf_op jit(solution)/shard_map/dot_general | solution.py:132
  455.6 18.0 %fusion.26 = f32[8,2,32,1024]{3,2,1,0:T(8,128)S(1)} fusion(bf16[8,2,32,1024]{3,2,1,0:T(8,128)(2,1)S(1)} %dot_general.43, s32[1024]{0:T(1024)S(1)} %get-tuple-element.21, s32[1024]{0:T(1024)S(1)} %get-tuple-element.20, s32[1024]{0:T(1024)S(1)} %get-tuple-element.22, s32[1024]{0:T(1024)S(1)} %get-tuple-element.19, pred[1024]{0:T(1024)(128)(4,1)S(1)} %fusion.85), kind=kOutput, calls=%fused_computation.42 | convolution fusion | flops 1094713344 | bytes 3163136 | tf_op jit(solution)/shard_map/dot_general | solution.py:132
  473.6 18.4 %slice.44 = f32[8,1,32,512]{3,2,1,0:T(8,128)} slice(f32[8,2,32,1024]{3,2,1,0:T(8,128)S(1)} %fusion.26), slice={[0:8:1], [0:1:1], [0:32:1], [0:1024:2]} | slice | bytes 1048576 | tf_op jit(solution)/shard_map/slice | solution.py:66
  492.0 18.4 %slice.45 = f32[8,1,32,512]{3,2,1,0:T(8,128)} slice(f32[8,2,32,1024]{3,2,1,0:T(8,128)S(1)} %fusion.26), slice={[0:8:1], [1:2:1], [0:32:1], [1:1024:2]} | slice | bytes 1048576 | tf_op jit(solution)/shard_map/slice | solution.py:66
  510.4 17.8 %slice.46 = f32[8,1,32,512]{3,2,1,0:T(8,128)S(1)} slice(f32[8,2,32,1024]{3,2,1,0:T(8,128)S(1)} %fusion.26), slice={[0:8:1], [0:1:1], [0:32:1], [1:1024:2]} | slice | bytes 1048576 | tf_op jit(solution)/shard_map/slice | solution.py:67
  528.3 18.1 %slice.47 = f32[8,1,32,512]{3,2,1,0:T(8,128)S(1)} slice(f32[8,2,32,1024]{3,2,1,0:T(8,128)S(1)} %fusion.26), slice={[0:8:1], [1:2:1], [0:32:1], [0:1024:2]} | slice | bytes 1048576 | tf_op jit(solution)/shard_map/slice | solution.py:67
  546.3 1.3 subtract_convert_fusion
  547.6 0.1 add_convert_fusion
  547.7 0.1 pad_maximum_fusion.2
  547.8 0.0 all-gather.6.cloned.1.call-done
  547.8 4.6 fusion.12
  552.4 7.3 %fusion.21 = bf16[8,1,512,512]{3,2,1,0:T(8,128)(2,1)} fusion(f32[8]{0:T(128)S(1)} %dynamic-slice_bitcast_fusion, f32[8,512,512]{2,0,1:T(8,128)S(1)} %fusion.12, bf16[8,512,64]{1,2,0:T(8,128)(2,1)S(1)} %bitcast.101, f32[512,32]{0,1:T(8,128)S(1)} %get-tuple-element.15, f32[512,32]{0,1:T(8,128)S(1)} %get-tuple-element.16, f32[64]{0:T(128)S(1)} %pad_maximum_fusion.4), kind=kOutput, calls=%fused_computation.38 | convolution fusion | flops 293699584 | bytes 13238560 | tf_op jit(solution)/shard_map/dot_general | solution.py:135
  (19 shorter events, 0.1 us)
Async XLA Ops:
  6.5 541.3 %copy-start = (bf16[1,16,16]{2,1,0:T(8,128)(2,1)S(1)}, bf16[1,16,16]{2,1,0:T(8,128)(2,1)}, u32[]{:S(2)}) copy-start(bf16[1,16,16]{2,1,0:T(8,128)(2,1)} %param.6) | copy-start | bytes 1540
  6.5 343.3 %reduce-scatter.2.cloned.1.call-start = ((), (), s32[]{:S(2)}) async-start(), calls=%async_computation.1 | async-start | bytes 9437184 | tf_op jit(solution)/shard_map/reduce_scatter | solution.py:122
  189.1 4.8 copy-start.1
  198.0 1.6 copy-start.2
  198.0 243.5 %all-gather.4.cloned.1.call-start = ((), (), s32[]{:S(2)}) async-start(), calls=%async_computation.2 | async-start | bytes 4718592 | tf_op jit(solution)/shard_map/all_gather | solution.py:126
  368.9 178.9 %all-gather.6.cloned.1.call-start = ((), (), s32[]{:S(2)}) async-start(), calls=%async_computation.3 | async-start | bytes 12582912 | tf_op jit(solution)/shard_map/all_gather | solution.py:104
  375.5 7.0 %copy-start.3 = (f32[1,16]{1,0:T(1,128)S(1)}, f32[1,16]{1,0:T(1,128)}, u32[]{:S(2)}) copy-start(f32[1,16]{1,0:T(1,128)} %param.7) | copy-start | bytes 196
Sparse Core Ops, SparseCore 0:
  198.1 151.6 reduce-scatter.1
  369.0 72.3 all-gather.3
  443.1 18.1 all-gather.5
where the time goes:
time: 575 us; the launch traced here: 567 us
  local copies, waits for them, and re-layouts  292 us (51%)
  waiting for transfers between devices  182 us (32%)
  matrix products  52.7 us (9%)
  other arithmetic  24.2 us (4%)
  between operations  13.6 us (2%)
    reduce_scatter x1, waiting for transfers between devices, on_device(): lax.psum_scatter(blocks, ('gx', 'gy'), scatter_dimension=0, tiled=True)[0]  123 us
    slice x2, local copies, waits for them, and re-layouts, split_flat(): real = shaped[:, 0, :, 0::2] + shaped[:, 1, :, 1::2]  73 us
    slice x2, local copies, waits for them, and re-layouts, split_flat(): imag = shaped[:, 1, :, 0::2] - shaped[:, 0, :, 1::2]  72.2 us
    all_gather x1, waiting for transfers between devices, on_device(): every = lax.all_gather(mixed[None], ('gx', 'gy'), axis=0, tiled=True)  58.8 us
    slice x2, local copies, waits for them, and re-layouts, join_flat(): real = shaped[:, 0, :, 0::2] - shaped[:, 1, :, 1::2]  36.8 us
    slice x2, local copies, waits for them, and re-layouts, join_flat(): imag = shaped[:, 0, :, 1::2] + shaped[:, 1, :, 0::2]  35.9 us
    slice x1, local copies, waits for them, and re-layouts, mix_modes(): w_imag = shaped[:, :, :, :, 1]  20.2 us
    dot_general x1, matrix products, on_device(): lax.dot_general(zhat.reshape(channels, planes, rows, 2 * KZ), table, (((1...  19.2 us
  transfers between devices with their start and end apart: 3, of which 2 were waited for; matrix products, arithmetic and copies ran while one was open for 26% of the time, Pallas kernels for 0%

commit v1 on v0

v1 whole, which is shorter than its diff:
```python
import functools
import math

import jax
import jax.numpy as jnp
import numpy as np
from jax import lax
from jax.experimental import pallas as pl
from jax.experimental.pallas import tpu as pltpu
from jax.sharding import PartitionSpec as P

CH = 16
KX = 32
KY = 32
KZ = 32
LANES = 128
MESH = pl.DeviceIdType.MESH
BF16 = jnp.bfloat16
F32 = jnp.float32


def rows_cols_dot(a, b):
    return lax.dot_general(a, b, (((1,), (1,)), ((), ())), preferred_element_type=F32)


def dot(a, b):
    return jnp.dot(a, b, preferred_element_type=F32)


def as_bf16(table):
    return jnp.asarray(np.asarray(table, np.float32).astype(jnp.bfloat16))


def angles(first, second, period):
    return ((first[:, None] * second[None, :]) % period) * (2.0 * math.pi / period)


def forward_z_table(zlen, count_y):
    angle = angles(np.arange(KZ), np.arange(zlen), zlen).reshape(count_y, -1, zlen)
    return as_bf16(np.stack([np.cos(angle), -np.sin(angle)], axis=1).reshape(2 * KZ, zlen))


def inverse_z_table(zlen):
    angle = angles(np.arange(KZ), np.arange(zlen), zlen)
    weight = np.where(np.arange(KZ) == 0, 1.0, 2.0)[:, None]
    return as_bf16(np.concatenate([weight * np.cos(angle), -weight * np.sin(angle)], axis=1))


def forward_y_table(count_y, rows):
    angle = angles(np.arange(count_y * rows), np.arange(KY) - KY // 2, count_y * rows)
    cosine, sine = np.cos(angle), np.sin(angle)
    parts = [np.concatenate([cosine, -sine], axis=1), np.concatenate([sine, cosine], axis=1)]
    nothing = np.zeros_like(parts[0])
    table = np.stack(
        [
            np.stack([np.concatenate([t, nothing], 1), np.concatenate([nothing, t], 1)])
            for t in parts
        ]
    )
    return as_bf16(table.reshape(2, 2, count_y, rows, LANES).transpose(2, 0, 1, 3, 4))


def inverse_y_table(count_y, rows):
    angle = angles(np.arange(count_y * rows), np.arange(KY) - KY // 2, count_y * rows)
    table = np.concatenate([np.cos(angle), np.sin(angle)], axis=1)
    return as_bf16(table.reshape(count_y, rows, 2 * KY))


def phase_scalars(count_x):
    angle = angles(np.arange(count_x), np.arange(KX) - KX // 2, count_x)
    return jnp.asarray(
        np.concatenate([np.cos(angle).reshape(-1), np.sin(angle).reshape(-1)]).astype(np.float32)
    )


def lane_tables():
    one = np.eye(KY)
    zero = np.zeros((KY, KY))
    half = np.block([[zero, -one], [one, zero]])
    turn = np.kron(np.eye(2), half)
    first = np.block([[one, zero], [zero, -one]])
    second = np.block([[zero, one], [one, zero]])
    wide = np.concatenate([first, first, second, second], axis=1)
    nothing = np.zeros_like(wide)
    spread = np.stack([np.concatenate([wide, nothing], 0), np.concatenate([nothing, wide], 0)])
    return as_bf16(turn), as_bf16(spread)


def row_tables(kz_each):
    table = np.zeros((2, kz_each * CH, 2 * 4 * kz_each))
    for half in range(2):
        for core in range(2):
            for low in range(4):
                for kz in range(kz_each):
                    channel = core * 8 + half * 4 + low
                    table[half, kz * CH + channel, (core * 4 + low) * kz_each + kz] = 1.0
    return as_bf16(table)


def modes_kernel(
    count_x,
    count_y,
    forward_scale,
    field_hbm,
    weights_hbm,
    fz_ref,
    ty_hbm,
    phase_ref,
    turn_ref,
    spread_ref,
    order_ref,
    other_hbm,
    m_ref,
    field_v,
    weights_v,
    ty_v,
    zs,
    sa,
    ra,
    rb,
    s_v,
    p1_v,
    p2_v,
    sc,
    rc,
    field_sem,
    weight_sem,
    ty_sem,
    fs_sem,
    fr_sem,
    as_sem,
    ar_sem,
    bs_sem,
    br_sem,
    cs_sem,
    cr_sem,
):
    mg = lax.axis_index("groups")
    mx = lax.axis_index("gx")
    my = lax.axis_index("gy")
    mz = lax.axis_index("gz")
    channels = field_v.shape[0]
    kz_each = KZ // count_y
    kx_each = KX // count_x
    classes = p1_v.shape[0]
    reps = kx_each // classes

    def device(dx, dy, dz):
        return (
            mg,
            lax.rem(mx + dx, count_x),
            lax.rem(my + dy, count_y),
            lax.rem(mz + dz, 2),
        )

    in_copies = [
        pltpu.make_async_copy(field_hbm.at[c, 0], field_v.at[c], field_sem.at[c])
        for c in range(channels)
    ]
    ty_copy = pltpu.make_async_copy(ty_hbm.at[my], ty_v, ty_sem)
    weight_copy = pltpu.make_async_copy(weights_hbm.at[0], weights_v, weight_sem)
    for copy in in_copies:
        copy.start()
    ty_copy.start()
    weight_copy.start()

    peers = [(0, dy, 0) for dy in range(1, count_y)]
    gather = [(dx, 0, dz) for dx in range(count_x) for dz in range(2) if (dx, dz) != (0, 0)]
    spread = [
        (dx, dy, 0) for dx in range(count_x) for dy in range(count_y) if (dx, dy) != (0, 0)
    ]
    everyone = sorted(set(peers) | set(gather) | set(spread))
    barrier = pltpu.get_barrier_semaphore()
    for offset in everyone:
        pl.semaphore_signal(barrier, inc=1, device_id=device(*offset), device_id_type=MESH)
    pl.semaphore_wait(barrier, len(everyone))

    field_sends = [
        pltpu.make_async_remote_copy(
            src_ref=field_hbm.at[c],
            dst_ref=other_hbm.at[c],
            send_sem=fs_sem.at[c],
            recv_sem=fr_sem.at[c],
            device_id=device(0, 0, 1),
            device_id_type=MESH,
        )
        for c in range(channels)
    ]
    for copy in field_sends:
        copy.start()

    for c in range(channels):
        in_copies[c].wait()
        zhat = rows_cols_dot(fz_ref[...], field_v[c])
        for d in range(count_y):
            for p in range(2):
                row = (d * 2 + p) * kz_each
                zs[d, p, c // 4, pl.ds((c % 4) * kz_each, kz_each), :] = zhat[
                    row : row + kz_each, :
                ]
    ty_copy.wait()
    for d in range(count_y):
        total = None
        for p in range(2):
            for h in range(2):
                term = dot(zs[d, p, h].astype(BF16), ty_v[p, h])
                total = term if total is None else total + term
        sa[d] = total.astype(BF16)

    def a_copy(dy):
        return pltpu.make_async_remote_copy(
            src_ref=sa.at[lax.rem(my + dy, count_y)],
            dst_ref=ra.at[dy],
            send_sem=as_sem.at[dy],
            recv_sem=ar_sem.at[dy],
            device_id=device(0, dy, 0),
            device_id_type=MESH,
        )

    a_copies = [a_copy(dy) for dy in range(1, count_y)]
    for copy in a_copies:
        copy.start()
    total = sa[my].astype(F32)
    for index, copy in enumerate(a_copies):
        copy.wait()
        total = total + ra[index + 1].astype(F32)
    rb[mx, mz] = total.astype(BF16)

    b_copies = [
        pltpu.make_async_remote_copy(
            src_ref=rb.at[mx, mz],
            dst_ref=rb.at[mx, mz],
            send_sem=bs_sem.at[dx, dz],
            recv_sem=br_sem.at[dx, dz],
            device_id=device(dx, 0, dz),
            device_id_type=MESH,
        )
        for dx, _, dz in gather
    ]
    for copy in b_copies:
        copy.start()
    for copy in b_copies:
        copy.wait()

    def phases(x, k):
        at = x * KX + mx * kx_each + k
        return phase_ref[at], phase_ref[count_x * KX + at]

    rows = 2 * 4 * kz_each
    sums = [None] * classes
    for x in range(count_x):
        block = rb[x].reshape(rows, LANES)
        turned = dot(block, turn_ref[...])
        block = block.astype(F32)
        for k in range(classes):
            cosine, sine = phases(x, k)
            term = block * cosine + turned * sine
            sums[k] = term if sums[k] is None else sums[k] + term
    for k in range(classes):
        spec = (sums[k] * forward_scale).astype(BF16)
        wide = dot(order_ref[0], dot(spec, spread_ref[0]).astype(BF16)) + dot(
            order_ref[1], dot(spec, spread_ref[1]).astype(BF16)
        )
        s_v[k] = wide.reshape(kz_each, CH, 2 * LANES)

    weight_copy.wait()
    copies = weights_v.shape[-1] // LANES

    def mix(kz, carry):
        for k in range(classes):
            weight = weights_v[k, kz].astype(F32)
            for r in range(1, reps):
                weight = weight + weights_v[k + r * classes, kz].astype(F32)
            both = s_v[k, kz]
            first = jnp.concatenate([both[:, :LANES]] * copies, axis=1)
            second = jnp.concatenate([both[:, LANES:]] * copies, axis=1)
            p1_v[k, pl.ds(kz, 1), :] = jnp.sum(weight * first, axis=0, keepdims=True)
            p2_v[k, pl.ds(kz, 1), :] = jnp.sum(weight * second, axis=0, keepdims=True)
        return carry

    lax.fori_loop(0, kz_each, mix, 0)

    width = weights_v.shape[-1]
    lane = lax.broadcasted_iota(jnp.int32, (kz_each, width), 1)
    is_real = lax.rem(lane, 2 * KY) < KY
    for x in range(count_x):
        real = imag = None
        for k in range(classes):
            cosine, sine = phases(x, k)
            first, second = p1_v[k], p2_v[k]
            re_term = first * cosine - second * sine
            im_term = second * cosine + first * sine
            real = re_term if real is None else real + re_term
            imag = im_term if imag is None else imag + im_term
        real = real + pltpu.roll(real, width - KY, 1)
        imag = imag + pltpu.roll(imag, KY, 1)
        sc[x] = jnp.where(is_real, real, imag).astype(BF16)

    c_copies = [
        pltpu.make_async_remote_copy(
            src_ref=sc.at[lax.rem(mx + dx, count_x)],
            dst_ref=rc.at[my, mx],
            send_sem=cs_sem.at[dx, dy],
            recv_sem=cr_sem.at[dx, dy],
            device_id=device(dx, dy, 0),
            device_id_type=MESH,
        )
        for dx, dy, _ in spread
    ]
    for copy in c_copies:
        copy.start()
    rc[my, mx] = sc[mx]
    for copy in c_copies:
        copy.wait()
    for d in range(count_y):
        total = rc[d, 0].astype(F32)
        for x in range(1, count_x):
            total = total + rc[d, x].astype(F32)
        m_ref[pl.ds(d * kz_each, kz_each), :] = total
    for copy in field_sends:
        copy.wait()


def modes(field, spectral, count_x, count_y):
    channels, planes, rows, zlen = field.shape
    kx_each, kz_each = spectral.shape[1], spectral.shape[2]
    width = spectral.shape[4]
    classes = count_x if kx_each % count_x == 0 else kx_each
    block = 4 * kz_each
    forward_scale = 1.0 / math.sqrt(count_x * count_y * rows * zlen)
    turn, spread = lane_tables()
    hbm = pl.BlockSpec(memory_space=pl.ANY)
    vmem = pl.BlockSpec(memory_space=pltpu.VMEM)
    smem = pl.BlockSpec(memory_space=pltpu.SMEM)
    dma = pltpu.SemaphoreType.DMA
    return pl.pallas_call(
        functools.partial(modes_kernel, count_x, count_y, forward_scale),
        out_shape=(
            jax.ShapeDtypeStruct(field.shape, BF16),
            jax.ShapeDtypeStruct((KZ, width), F32),
        ),
        in_specs=[hbm, hbm, vmem, hbm, smem, vmem, vmem, vmem],
        out_specs=(hbm, vmem),
        scratch_shapes=[
            pltpu.VMEM((channels, rows, zlen), BF16),
            pltpu.VMEM(spectral.shape[1:], BF16),
            pltpu.VMEM((2, 2, rows, LANES), BF16),
            pltpu.VMEM((count_y, 2, 2, block, rows), F32),
            pltpu.VMEM((count_y, block, LANES), BF16),
            pltpu.VMEM((count_y, block, LANES), BF16),
            pltpu.VMEM((count_x, 2, block, LANES), BF16),
            pltpu.VMEM((classes, kz_each, CH, 2 * LANES), F32),
            pltpu.VMEM((classes, kz_each, width), F32),
            pltpu.VMEM((classes, kz_each, width), F32),
            pltpu.VMEM((count_x, kz_each, width), BF16),
            pltpu.VMEM((count_y, count_x, kz_each, width), BF16),
            dma((channels,)),
            dma,
            dma,
            dma((channels,)),
            dma((channels,)),
            dma((count_y,)),
            dma((count_y,)),
            dma((count_x, 2)),
            dma((count_x, 2)),
            dma((count_x, count_y)),
            dma((count_x, count_y)),
        ],
        compiler_params=pltpu.CompilerParams(
            collective_id=0, has_side_effects=True, vmem_limit_bytes=40 * 1024 * 1024
        ),
        name="modes",
    )(
        field,
        spectral,
        forward_z_table(zlen, count_y),
        forward_y_table(count_y, rows),
        phase_scalars(count_x),
        turn,
        spread,
        row_tables(kz_each),
    )


def cells_kernel(
    inverse_scale, strip, field_ref, other_ref, m_ref, gz_ref, ty_ref, point_ref, shift_ref,
    out_ref, g_v, mix_v,
):
    my = lax.axis_index("gy")
    mz = lax.axis_index("gz")
    channels, _, rows, zlen = field_ref.shape
    step = pl.program_id(0)

    @pl.when(step == 0)
    def _():
        lines = jnp.transpose(m_ref[...]).astype(BF16)
        both = dot(lines, gz_ref[...]) * inverse_scale
        both = both.reshape(channels, 2, KY, 2 * zlen)
        re, im = both[:, 0], both[:, 1]
        g_v[:, :KY, :] = (re[..., :zlen] + im[..., zlen:]).astype(BF16)
        g_v[:, KY:, :] = (re[..., zlen:] - im[..., :zlen]).astype(BF16)

        tall, wide = channels * strip, CH * strip
        pick_row = lax.broadcasted_iota(jnp.int32, (tall, CH), 0) // strip + mz * channels
        left = (pick_row == lax.broadcasted_iota(jnp.int32, (tall, CH), 1)).astype(F32)
        pick_col = lax.rem(
            lax.broadcasted_iota(jnp.int32, (CH, wide), 1) // strip + mz * channels, CH
        )
        right = (pick_col == lax.broadcasted_iota(jnp.int32, (CH, wide), 0)).astype(F32)
        filled = dot(dot(left.astype(BF16), point_ref[0]).astype(BF16), right.astype(BF16))
        at_row = lax.rem(lax.broadcasted_iota(jnp.int32, (tall, wide), 0), strip)
        at_col = lax.rem(lax.broadcasted_iota(jnp.int32, (tall, wide), 1), strip)
        mix_v[...] = jnp.where(at_row == at_col, filled, 0.0).astype(BF16)

    def one_strip(s, carry):
        cells = pl.ds(pl.multiple_of(s * strip, strip), strip)
        own = field_ref[:, 0, cells, :].reshape(channels * strip, zlen)
        other = other_ref[:, 0, cells, :].reshape(channels * strip, zlen)
        local = dot(mix_v[...], jnp.concatenate([own, other], axis=0))
        waves = ty_ref[my, pl.ds(pl.multiple_of(step * rows + s * strip, strip), strip), :]
        for o in range(channels):
            x = dot(waves, g_v[o]) + local[o * strip : (o + 1) * strip]
            x = x + shift_ref[0, mz * channels + o]
            inner = x * (0.7978845608028654 + 0.035677408136300125 * (x * x))
            half = 0.5 * x
            out_ref[o, 0, cells, :] = (half + half * jnp.tanh(inner)).astype(BF16)
        return carry

    lax.fori_loop(0, rows // strip, one_strip, 0)


def cells(field, other, lines, pointwise, shift, count_y):
    channels, planes, rows, zlen = field.shape
    inverse_scale = 1.0 / math.sqrt(2 * KX * KY * KZ)
    tile = min(rows, 64)
    strip = 16
    slab = pl.BlockSpec((channels, 1, tile, zlen), lambda i: (0, 0, i, 0))
    vmem = pl.BlockSpec(memory_space=pltpu.VMEM)
    smem = pl.BlockSpec(memory_space=pltpu.SMEM)
    return pl.pallas_call(
        functools.partial(cells_kernel, inverse_scale, strip),
        grid=(rows // tile,),
        out_shape=jax.ShapeDtypeStruct(field.shape, BF16),
        in_specs=[slab, slab, vmem, vmem, vmem, vmem, smem],
        out_specs=slab,
        scratch_shapes=[
            pltpu.VMEM((channels, 2 * KY, zlen), BF16),
            pltpu.VMEM((channels * strip, CH * strip), BF16),
        ],
        compiler_params=pltpu.CompilerParams(vmem_limit_bytes=40 * 1024 * 1024),
        name="cells",
    )(
        field,
        other,
        lines,
        inverse_z_table(zlen),
        inverse_y_table(count_y, rows),
        pointwise,
        shift,
    )


def on_device(field, spectral, pointwise, shift):
    count_x = lax.axis_size("gx")
    count_y = lax.axis_size("gy")
    for layer in range(spectral.shape[0]):
        other, lines = modes(field, spectral[layer : layer + 1], count_x, count_y)
        field = cells(
            field, other, lines, pointwise[layer : layer + 1], shift[layer : layer + 1], count_y
        )
    return field


def solution(mesh):
    return jax.shard_map(
        on_device,
        mesh=mesh,
        in_specs=(P("gz", ("groups", "gx"), "gy", None), P(None, "gx", "gy", None, "gz"), P(), P()),
        out_specs=P("gz", ("groups", "gx"), "gy", None),
        check_vma=False,
    )
```

time: 575 us -> 45.7 us (0.08); the launches traced: 567 us -> 45.3 us
  local copies, waits for them, and re-layouts: 292 us -> 9.1 us
  waiting for transfers between devices: 182 us -> 0 us
  matrix products: 52.7 us -> 0 us
  Pallas kernels: 0 us -> 36.2 us
  other arithmetic: 24.2 us -> 0 us
  between operations: 13.6 us -> 0.05 us
    slice x9 -> x0, local copies, waits for them, and re-layouts: 238 us -> none  [the longest x2 73 us: split_flat(): real = shaped[:, 0, :, 0::2] + shaped[:, 1, :, 1::2]]
    reduce_scatter x1 -> x0, waiting for transfers between devices: 123 us -> none  [on_device(): lax.psum_scatter(blocks, ('gx', 'gy'), scatter_dimension=0, tiled=True)[0]]
    all_gather x2 -> x0, waiting for transfers between devices: 58.9 us -> none  [the longest x1 58.8 us: on_device(): every = lax.all_gather(mixed[None], ('gx', 'gy'), axis=0, tiled=True)]
    dot_general x5 -> x0, matrix products: 52.7 us -> none  [the longest x1 19.2 us: on_device(): lax.dot_general(zhat.reshape(channels, planes, rows, 2 * KZ), table, (((1...]
    pallas_call x0 -> x2, Pallas kernels: none -> 36.2 us  [the longest x1 24.1 us: modes(): pl.pallas_call(functools.partial(modes_kernel, count_x, count_y, forward_...]
    another operation x5 -> x0, local copies, waits for them, and re-layouts: 23.9 us -> none  [the longest x4 16.8 us: split_flat(): return jnp.stack([real, imag], axis=1).reshape(channels, 2, kcount, KX, KY)]
    dot_general x1 -> x0, other arithmetic: 13.8 us -> none  [mix_modes(): jnp.einsum('abiok,abik->abok', w_real, s_real, preferred_element_type=jnp...]
    dot_general x2 -> x0, local copies, waits for them, and re-layouts: 7.24 us -> none  [the longest x1 7.08 us: on_device(): prod = jnp.dot(flat, back, preferred_element_type=jnp.float32)]
  transfers between devices with their start and end apart: 3 -> 0, of which waited for: 2 -> 0; matrix products, arithmetic and copies ran while one was open for 26% -> 0% of each run, Pallas kernels for 0% -> 0%
where the time goes in v1:
time: 45.7 us; the launch traced here: 45.3 us
  Pallas kernels  36.2 us (79%)
  local copies, waits for them, and re-layouts  9.1 us (20%)
    pallas_call x1, Pallas kernels, modes(): pl.pallas_call(functools.partial(modes_kernel, count_x, count_y, forward_...  24.1 us
    pallas_call x1, Pallas kernels, cells(): pl.pallas_call(functools.partial(cells_kernel, inverse_scale, strip), gri...  12.1 us
    unnamed x24, local copies, waits for them, and re-layouts  9.1 us

profile of v1, /device:TPU:0, one launch (start us, length us, event | category | flops | bytes accessed | tf_op | source)
XLA Modules:
  0.0 45.3 jit_solution(62394739802190115)
XLA Ops:
  0.0 0.0 copy-start
  0.0 2.2 %copy-done = bf16[8,1,512,512]{3,2,1,0:T(8,128)(2,1)S(1)} copy-done((bf16[8,1,512,512]{3,2,1,0:T(8,128)(2,1)S(1)}, bf16[8,1,512,512]{3,2,1,0:T(8,128)(2,1)}, u32[]{:S(2)}) %copy-start) | copy-done | bytes 4194328
  2.2 0.0 copy-start.1
  2.2 1.6 %copy-done.1 = bf16[1,8,16,16,512]{4,3,2,1,0:T(8,128)(2,1)S(1)} copy-done((bf16[1,8,16,16,512]{4,3,2,1,0:T(8,128)(2,1)S(1)}, bf16[1,8,16,16,512]{4,3,2,1,0:T(8,128)(2,1)}, u32[]{:S(2)}) %copy-start.1) | copy-done | bytes 2097176
  3.8 0.0 copy-start.2
  3.8 1.2 %copy-done.2 = bf16[2,2,2,512,128]{4,3,2,1,0:T(8,128)(2,1)S(1)} copy-done((bf16[2,2,2,512,128]{4,3,2,1,0:T(8,128)(2,1)S(1)}, bf16[2,2,2,512,128]{4,3,2,1,0:T(8,128)(2,1)}, u32[]{:S(2)}) %copy-start.2) | copy-done | bytes 1048600
  5.0 0.0 copy-start.4
  5.0 0.9 %copy-done.4 = bf16[2,256,128]{2,1,0:T(8,128)(2,1)S(1)} copy-done((bf16[2,256,128]{2,1,0:T(8,128)(2,1)S(1)}, bf16[2,256,128]{2,1,0:T(8,128)(2,1)}, u32[]{:S(2)}) %copy-start.4) | copy-done | bytes 131096
  5.9 0.0 copy-start.5
  5.9 0.9 %copy-done.5 = bf16[2,128,256]{2,1,0:T(8,128)(2,1)S(1)} copy-done((bf16[2,128,256]{2,1,0:T(8,128)(2,1)S(1)}, bf16[2,128,256]{2,1,0:T(8,128)(2,1)}, u32[]{:S(2)}) %copy-start.5) | copy-done | bytes 131096
  6.8 0.0 copy-start.7
  6.8 0.8 %copy-done.7 = bf16[64,512]{1,0:T(8,128)(2,1)S(1)} copy-done((bf16[64,512]{1,0:T(8,128)(2,1)S(1)}, bf16[64,512]{1,0:T(8,128)(2,1)}, u32[]{:S(2)}) %copy-start.7) | copy-done | bytes 65560
  7.7 0.0 copy-start.8
  7.7 0.8 %copy-done.8 = bf16[128,128]{1,0:T(8,128)(2,1)S(1)} copy-done((bf16[128,128]{1,0:T(8,128)(2,1)S(1)}, bf16[128,128]{1,0:T(8,128)(2,1)}, u32[]{:S(2)}) %copy-start.8) | copy-done | bytes 32792
  8.4 0.0 copy-start.10
  8.4 0.7 %copy-done.10 = f32[256]{0:T(256)S(1)} copy-done((f32[256]{0:T(256)S(1)}, f32[256]{0:T(256)}, u32[]{:S(2)}) %copy-start.10) | copy-done | bytes 1048
  9.1 0.0 copy-start.3
  9.1 0.0 copy-start.6
  9.1 0.0 copy-start.9
  9.1 0.0 copy-start.11
  9.1 24.1 %modes.1 = (bf16[8,1,512,512]{3,2,1,0:T(8,128)(2,1)S(1)}, f32[32,512]{1,0:T(8,128)S(1)}) custom-call(bf16[8,1,512,512]{3,2,1,0:T(8,128)(2,1)S(1)} %copy-done, bf16[1,8,16,16,512]{4,3,2,1,0:T(8,128)(2,1)S(1)} %copy-done.1, bf16[64,512]{1,0:T(8,128)(2,1)S(1)} %copy-done.7, bf16[2,2,2,512,128]{4,3,2,1,0:T(8,128)(2,1)S(1)} %copy-done.2, f32[256]{0:T(256)S(1)} %copy-done.10, ...), custom_call_target="tpu_custom_call" | custom-call | tf_op jit(solution)/shard_map/modes/pallas_call | solution.py:336
  33.2 0.0 copy-done.3
  33.2 0.0 copy-done.6
  33.2 0.0 copy-done.9
  33.3 0.0 copy-done.11
  33.3 12.1 %cells.1 = bf16[8,1,512,512]{3,2,1,0:T(8,128)(2,1)} custom-call(bf16[8,1,512,512]{3,2,1,0:T(8,128)(2,1)S(1)} %copy-done, bf16[8,1,512,512]{3,2,1,0:T(8,128)(2,1)S(1)} %get-tuple-element.7.other_ref, f32[32,512]{1,0:T(8,128)S(1)} %get-tuple-element.8.m_ref, bf16[32,1024]{1,0:T(8,128)(2,1)S(1)} %copy-done.6, bf16[2,512,64]{2,1,0:T(8,128)(2,1)S(1)} %copy-done.3, ...), custom_call_target="tpu_custom_call" | custom-call | tf_op jit(solution)/shard_map/cells/pallas_call | solution.py:440
Async XLA Ops:
  0.0 2.2 %copy-start = (bf16[8,1,512,512]{3,2,1,0:T(8,128)(2,1)S(1)}, bf16[8,1,512,512]{3,2,1,0:T(8,128)(2,1)}, u32[]{:S(2)}) copy-start(bf16[8,1,512,512]{3,2,1,0:T(8,128)(2,1)} %field_ref.1) | copy-start | bytes 12582916
  2.2 1.6 %copy-start.1 = (bf16[1,8,16,16,512]{4,3,2,1,0:T(8,128)(2,1)S(1)}, bf16[1,8,16,16,512]{4,3,2,1,0:T(8,128)(2,1)}, u32[]{:S(2)}) copy-start(bf16[1,8,16,16,512]{4,3,2,1,0:T(8,128)(2,1)} %weights_hbm.1) | copy-start | bytes 6291460
  3.8 1.2 %copy-start.2 = (bf16[2,2,2,512,128]{4,3,2,1,0:T(8,128)(2,1)S(1)}, bf16[2,2,2,512,128]{4,3,2,1,0:T(8,128)(2,1)}, u32[]{:S(2)}) copy-start(bf16[2,2,2,512,128]{4,3,2,1,0:T(8,128)(2,1)} %constant.19.clone.ty_hbm) | copy-start | bytes 3145732
  5.0 0.9 %copy-start.4 = (bf16[2,256,128]{2,1,0:T(8,128)(2,1)S(1)}, bf16[2,256,128]{2,1,0:T(8,128)(2,1)}, u32[]{:S(2)}) copy-start(bf16[2,256,128]{2,1,0:T(8,128)(2,1)} %constant.21.clone.order_ref) | copy-start | bytes 393220
  5.9 0.9 %copy-start.5 = (bf16[2,128,256]{2,1,0:T(8,128)(2,1)S(1)}, bf16[2,128,256]{2,1,0:T(8,128)(2,1)}, u32[]{:S(2)}) copy-start(bf16[2,128,256]{2,1,0:T(8,128)(2,1)} %constant.17.clone.spread_ref) | copy-start | bytes 393220
  6.8 0.8 %copy-start.7 = (bf16[64,512]{1,0:T(8,128)(2,1)S(1)}, bf16[64,512]{1,0:T(8,128)(2,1)}, u32[]{:S(2)}) copy-start(bf16[64,512]{1,0:T(8,128)(2,1)} %constant.18.clone.fz_ref) | copy-start | bytes 196612
  7.7 0.8 %copy-start.8 = (bf16[128,128]{1,0:T(8,128)(2,1)S(1)}, bf16[128,128]{1,0:T(8,128)(2,1)}, u32[]{:S(2)}) copy-start(bf16[128,128]{1,0:T(8,128)(2,1)} %constant.16.clone.turn_ref) | copy-start | bytes 98308
  8.4 0.7 %copy-start.10 = (f32[256]{0:T(256)S(1)}, f32[256]{0:T(256)}, u32[]{:S(2)}) copy-start(f32[256]{0:T(256)} %constant.20.clone.phase_ref) | copy-start | bytes 3076
  9.1 24.1 %copy-start.3 = (bf16[2,512,64]{2,1,0:T(8,128)(2,1)S(1)}, bf16[2,512,64]{2,1,0:T(8,128)(2,1)}, u32[]{:S(2)}) copy-start(bf16[2,512,64]{2,1,0:T(8,128)(2,1)} %constant.23.clone.ty_ref) | copy-start | bytes 393220
  9.1 24.1 %copy-start.6 = (bf16[32,1024]{1,0:T(8,128)(2,1)S(1)}, bf16[32,1024]{1,0:T(8,128)(2,1)}, u32[]{:S(2)}) copy-start(bf16[32,1024]{1,0:T(8,128)(2,1)} %constant.22.clone.gz_ref) | copy-start | bytes 196612
  9.1 24.1 %copy-start.9 = (bf16[1,16,16]{2,1,0:T(8,128)(2,1)S(1)}, bf16[1,16,16]{2,1,0:T(8,128)(2,1)}, u32[]{:S(2)}) copy-start(bf16[1,16,16]{2,1,0:T(8,128)(2,1)} %point_ref.1) | copy-start | bytes 1540
  9.1 24.2 %copy-start.11 = (f32[1,16]{1,0:T(1,128)S(1)}, f32[1,16]{1,0:T(1,128)}, u32[]{:S(2)}) copy-start(f32[1,16]{1,0:T(1,128)} %shift_ref.1) | copy-start | bytes 196

commit v2 on v1

--- a/solution.py
+++ b/solution.py
@@ -14,6 +14,7 @@
 KY = 32
 KZ = 32
 LANES = 128
+VMEM_BYTES = 60 * 1024 * 1024
 MESH = pl.DeviceIdType.MESH
 BF16 = jnp.bfloat16
 F32 = jnp.float32
@@ -28,7 +29,7 @@
 
 
 def as_bf16(table):
-    return jnp.asarray(np.asarray(table, np.float32).astype(jnp.bfloat16))
+    return np.asarray(table, np.float32).astype(jnp.bfloat16)
 
 
 def angles(first, second, period):
@@ -66,11 +67,11 @@
     return as_bf16(table.reshape(count_y, rows, 2 * KY))
 
 
-def phase_scalars(count_x):
+def phase_rows(count_x):
     angle = angles(np.arange(count_x), np.arange(KX) - KX // 2, count_x)
-    return jnp.asarray(
-        np.concatenate([np.cos(angle).reshape(-1), np.sin(angle).reshape(-1)]).astype(np.float32)
-    )
+    both = np.stack([np.cos(angle), np.sin(angle)], axis=-1)
+    both = both.reshape(count_x, count_x, -1).transpose(1, 0, 2).reshape(count_x, -1, 1)
+    return as_bf16(np.broadcast_to(both, both.shape[:2] + (LANES,)))
 
 
 def lane_tables():
@@ -97,23 +98,32 @@
     return as_bf16(table)
 
 
+def in_lanes(table):
+    return np.concatenate(np.split(table, table.shape[-1] // LANES, axis=-1), axis=-2)
+
+
 def modes_kernel(
     count_x,
     count_y,
     forward_scale,
     field_hbm,
     weights_hbm,
-    fz_ref,
-    ty_hbm,
-    phase_ref,
-    turn_ref,
-    spread_ref,
-    order_ref,
-    other_hbm,
+    table_hbm,
+    point_hbm,
+    local_hbm,
     m_ref,
     field_v,
+    other_v,
     weights_v,
     ty_v,
+    fz_v,
+    phase_v,
+    turn_v,
+    spread_v,
+    order_v,
+    point_v,
+    mix_v,
+    local_v,
     zs,
     sa,
     ra,
@@ -125,7 +135,8 @@
     rc,
     field_sem,
     weight_sem,
-    ty_sem,
+    table_sem,
+    local_sem,
     fs_sem,
     fr_sem,
     as_sem,
@@ -139,7 +150,7 @@
     mx = lax.axis_index("gx")
     my = lax.axis_index("gy")
     mz = lax.axis_index("gz")
-    channels = field_v.shape[0]
+    channels, rows, zlen = field_v.shape
     kz_each = KZ // count_y
     kx_each = KX // count_x
     classes = p1_v.shape[0]
@@ -157,11 +168,29 @@
         pltpu.make_async_copy(field_hbm.at[c, 0], field_v.at[c], field_sem.at[c])
         for c in range(channels)
     ]
-    ty_copy = pltpu.make_async_copy(ty_hbm.at[my], ty_v, ty_sem)
     weight_copy = pltpu.make_async_copy(weights_hbm.at[0], weights_v, weight_sem)
+    small = []
+    place = 0
+    for target, owner, owners in (
+        (fz_v, 0, 1),
+        (ty_v, my, count_y),
+        (turn_v, 0, 1),
+        (phase_v, mx, count_x),
+        (spread_v, 0, 1),
+        (order_v, 0, 1),
+    ):
+        size = target.shape[0]
+        source = table_hbm.at[pl.ds(pl.multiple_of(place + owner * size, 16), size)]
+        small.append(pltpu.make_async_copy(source, target, table_sem.at[len(small)]))
+        place += owners * size
+    small.append(pltpu.make_async_copy(point_hbm.at[0], point_v, table_sem.at[len(small)]))
+    fz_copy, ty_copy, *table_copies = small
+    fz_copy.start()
     for copy in in_copies:
         copy.start()
     ty_copy.start()
+    for copy in table_copies:
+        copy.start()
     weight_copy.start()
 
     peers = [(0, dy, 0) for dy in range(1, count_y)]
@@ -173,12 +202,13 @@
     barrier = pltpu.get_barrier_semaphore()
     for offset in everyone:
         pl.semaphore_signal(barrier, inc=1, device_id=device(*offset), device_id_type=MESH)
-    pl.semaphore_wait(barrier, len(everyone))
-
+
+    fz_copy.wait()
+    fz = jnp.concatenate(jnp.split(fz_v[...], zlen // LANES, axis=0), axis=1)
     field_sends = [
         pltpu.make_async_remote_copy(
-            src_ref=field_hbm.at[c],
-            dst_ref=other_hbm.at[c],
+            src_ref=field_hbm.at[c, 0],
+            dst_ref=other_v.at[c],
             send_sem=fs_sem.at[c],
             recv_sem=fr_sem.at[c],
             device_id=device(0, 0, 1),
@@ -186,12 +216,13 @@
         )
         for c in range(channels)
     ]
-    for copy in field_sends:
-        copy.start()
-
     for c in range(channels):
+        if c == channels // 2:
+            pl.semaphore_wait(barrier, len(everyone))
+            for copy in field_sends:
+                copy.start()
         in_copies[c].wait()
-        zhat = rows_cols_dot(fz_ref[...], field_v[c])
+        zhat = rows_cols_dot(fz, field_v[c])
         for d in range(count_y):
             for p in range(2):
                 row = (d * 2 + p) * kz_each
@@ -203,7 +234,7 @@
         total = None
         for p in range(2):
             for h in range(2):
-                term = dot(zs[d, p, h].astype(BF16), ty_v[p, h])
+                term = dot(zs[d, p, h].astype(BF16), ty_v[pl.ds((p * 2 + h) * rows, rows), :])
                 total = term if total is None else total + term
         sa[d] = total.astype(BF16)
 
@@ -242,15 +273,22 @@
     for copy in b_copies:
         copy.wait()
 
+    for copy in table_copies:
+        copy.wait()
+
+    phase = phase_v[...].astype(F32)
+
     def phases(x, k):
-        at = x * KX + mx * kx_each + k
-        return phase_ref[at], phase_ref[count_x * KX + at]
-
-    rows = 2 * 4 * kz_each
+        at = 2 * (x * kx_each + k)
+        return phase[at : at + 1], phase[at + 1 : at + 2]
+
+    block_rows = 2 * 4 * kz_each
+    spread_rows = spread_v.shape[0] // 4
+    order_rows = kz_each * CH
     sums = [None] * classes
     for x in range(count_x):
-        block = rb[x].reshape(rows, LANES)
-        turned = dot(block, turn_ref[...])
+        block = rb[x].reshape(block_rows, LANES)
+        turned = dot(block, turn_v[...])
         block = block.astype(F32)
         for k in range(classes):
             cosine, sine = phases(x, k)
@@ -258,9 +296,15 @@
             sums[k] = term if sums[k] is None else sums[k] + term
     for k in range(classes):
         spec = (sums[k] * forward_scale).astype(BF16)
-        wide = dot(order_ref[0], dot(spec, spread_ref[0]).astype(BF16)) + dot(
-            order_ref[1], dot(spec, spread_ref[1]).astype(BF16)
-        )
+        wide = None
+        for half in range(2):
+            parts = [
+                dot(spec, spread_v[pl.ds((half * 2 + t) * spread_rows, spread_rows), :])
+                for t in range(2)
+            ]
+            order = order_v[pl.ds(half * order_rows, order_rows), :block_rows]
+            term = dot(order, jnp.concatenate(parts, axis=1).astype(BF16))
+            wide = term if wide is None else wide + term
         s_v[k] = wide.reshape(kz_each, CH, 2 * LANES)
 
     weight_copy.wait()
@@ -286,7 +330,7 @@
     for x in range(count_x):
         real = imag = None
         for k in range(classes):
-            cosine, sine = phases(x, k)
+            cosine, sine = (jnp.concatenate([t] * copies, axis=1) for t in phases(x, k))
             first, second = p1_v[k], p2_v[k]
             re_term = first * cosine - second * sine
             im_term = second * cosine + first * sine
@@ -310,6 +354,41 @@
     for copy in c_copies:
         copy.start()
     rc[my, mx] = sc[mx]
+
+    tall, wide = mix_v.shape
+    strip = tall // channels
+    pick_row = lax.broadcasted_iota(jnp.int32, (tall, CH), 0) // strip + mz * channels
+    left = (pick_row == lax.broadcasted_iota(jnp.int32, (tall, CH), 1)).astype(F32)
+    pick_col = lax.rem(
+        lax.broadcasted_iota(jnp.int32, (CH, wide), 1) // strip + mz * channels, CH
+    )
+    right = (pick_col == lax.broadcasted_iota(jnp.int32, (CH, wide), 0)).astype(F32)
+    at_row = lax.rem(lax.broadcasted_iota(jnp.int32, (tall, wide), 0), strip)
+    at_col = lax.rem(lax.broadcasted_iota(jnp.int32, (tall, wide), 1), strip)
+    filled = dot(dot(left.astype(BF16), point_v[...]).astype(BF16), right.astype(BF16))
+    mix_v[...] = jnp.where(at_row == at_col, 0.5 * filled, 0.0).astype(BF16)
+    for copy in field_sends:
+        copy.wait()
+
+    tile = 4 * strip
+
+    def local_copy(i):
+        cells = pl.ds(pl.multiple_of(i * tile, tile), tile)
+        return pltpu.make_async_copy(
+            local_v.at[:, cells, :], local_hbm.at[:, cells, :], local_sem.at[i]
+        )
+
+    def pointwise_tile(i, carry):
+        for part in range(tile // strip):
+            cells = pl.ds(pl.multiple_of(i * tile + part * strip, strip), strip)
+            own = field_v[:, cells, :].reshape(channels * strip, zlen)
+            other = other_v[:, cells, :].reshape(channels * strip, zlen)
+            local = dot(mix_v[...], jnp.concatenate([own, other], axis=0)).astype(BF16)
+            local_v[:, cells, :] = local.reshape(channels, strip, zlen)
+        local_copy(i).start()
+        return carry
+
+    lax.fori_loop(0, rows // tile, pointwise_tile, 0)
     for copy in c_copies:
         copy.wait()
     for d in range(count_y):
@@ -317,34 +396,54 @@
         for x in range(1, count_x):
             total = total + rc[d, x].astype(F32)
         m_ref[pl.ds(d * kz_each, kz_each), :] = total
-    for copy in field_sends:
-        copy.wait()
-
-
-def modes(field, spectral, count_x, count_y):
+    for i in range(rows // tile):
+        local_copy(i).wait()
+
+
+def modes(field, spectral, pointwise, count_x, count_y):
     channels, planes, rows, zlen = field.shape
     kx_each, kz_each = spectral.shape[1], spectral.shape[2]
     width = spectral.shape[4]
     classes = count_x if kx_each % count_x == 0 else kx_each
     block = 4 * kz_each
+    strip = 16
     forward_scale = 1.0 / math.sqrt(count_x * count_y * rows * zlen)
     turn, spread = lane_tables()
+    order = row_tables(kz_each)
+    order = np.pad(order, ((0, 0), (0, 0), (0, LANES - order.shape[-1])))
+    tables = [
+        in_lanes(forward_z_table(zlen, count_y)),
+        forward_y_table(count_y, rows),
+        turn,
+        phase_rows(count_x),
+        in_lanes(spread),
+        order,
+    ]
+    table = jnp.asarray(np.concatenate([t.reshape(-1, LANES) for t in tables]))
     hbm = pl.BlockSpec(memory_space=pl.ANY)
     vmem = pl.BlockSpec(memory_space=pltpu.VMEM)
-    smem = pl.BlockSpec(memory_space=pltpu.SMEM)
     dma = pltpu.SemaphoreType.DMA
     return pl.pallas_call(
         functools.partial(modes_kernel, count_x, count_y, forward_scale),
         out_shape=(
-            jax.ShapeDtypeStruct(field.shape, BF16),
+            jax.ShapeDtypeStruct((channels, rows, zlen), BF16),
             jax.ShapeDtypeStruct((KZ, width), F32),
         ),
-        in_specs=[hbm, hbm, vmem, hbm, smem, vmem, vmem, vmem],
+        in_specs=[hbm, hbm, hbm, hbm],
         out_specs=(hbm, vmem),
         scratch_shapes=[
             pltpu.VMEM((channels, rows, zlen), BF16),
+            pltpu.VMEM((channels, rows, zlen), BF16),
             pltpu.VMEM(spectral.shape[1:], BF16),
-            pltpu.VMEM((2, 2, rows, LANES), BF16),
+            pltpu.VMEM((4 * rows, LANES), BF16),
+            pltpu.VMEM((2 * KZ * (zlen // LANES), LANES), BF16),
+            pltpu.VMEM((count_x * kx_each * 2, LANES), BF16),
+            pltpu.VMEM(turn.shape, BF16),
+            pltpu.VMEM((4 * LANES, LANES), BF16),
+            pltpu.VMEM((2 * kz_each * CH, LANES), BF16),
+            pltpu.VMEM(pointwise.shape[1:], BF16),
+            pltpu.VMEM((channels * strip, CH * strip), BF16),
+            pltpu.VMEM((channels, rows, zlen), BF16),
             pltpu.VMEM((count_y, 2, 2, block, rows), F32),
             pltpu.VMEM((count_y, block, LANES), BF16),
             pltpu.VMEM((count_y, block, LANES), BF16),
@@ -356,7 +455,8 @@
             pltpu.VMEM((count_y, count_x, kz_each, width), BF16),
             dma((channels,)),
             dma,
-            dma,
+            dma((7,)),
+            dma((rows // (4 * strip),)),
             dma((channels,)),
             dma((channels,)),
             dma((count_y,)),
@@ -367,95 +467,91 @@
             dma((count_x, count_y)),
         ],
         compiler_params=pltpu.CompilerParams(
-            collective_id=0, has_side_effects=True, vmem_limit_bytes=40 * 1024 * 1024
+            collective_id=0, has_side_effects=True, vmem_limit_bytes=VMEM_BYTES
         ),
         name="modes",
-    )(
-        field,
-        spectral,
-        forward_z_table(zlen, count_y),
-        forward_y_table(count_y, rows),
-        phase_scalars(count_x),
-        turn,
-        spread,
-        row_tables(kz_each),
-    )
+    )(field, spectral, table, pointwise)
 
 
 def cells_kernel(
-    inverse_scale, strip, field_ref, other_ref, m_ref, gz_ref, ty_ref, point_ref, shift_ref,
-    out_ref, g_v, mix_v,
+    inverse_scale, local_hbm, m_hbm, gz_hbm, ty_hbm, shift_ref, out_hbm,
+    local_v, m_v, gz_v, ty_v, out_v, g_v, small_sem, local_sem, out_sem,
 ):
     my = lax.axis_index("gy")
     mz = lax.axis_index("gz")
-    channels, _, rows, zlen = field_ref.shape
-    step = pl.program_id(0)
-
-    @pl.when(step == 0)
-    def _():
-        lines = jnp.transpose(m_ref[...]).astype(BF16)
-        both = dot(lines, gz_ref[...]) * inverse_scale
-        both = both.reshape(channels, 2, KY, 2 * zlen)
-        re, im = both[:, 0], both[:, 1]
-        g_v[:, :KY, :] = (re[..., :zlen] + im[..., zlen:]).astype(BF16)
-        g_v[:, KY:, :] = (re[..., zlen:] - im[..., :zlen]).astype(BF16)
-
-        tall, wide = channels * strip, CH * strip
-        pick_row = lax.broadcasted_iota(jnp.int32, (tall, CH), 0) // strip + mz * channels
-        left = (pick_row == lax.broadcasted_iota(jnp.int32, (tall, CH), 1)).astype(F32)
-        pick_col = lax.rem(
-            lax.broadcasted_iota(jnp.int32, (CH, wide), 1) // strip + mz * channels, CH
-        )
-        right = (pick_col == lax.broadcasted_iota(jnp.int32, (CH, wide), 0)).astype(F32)
-        filled = dot(dot(left.astype(BF16), point_ref[0]).astype(BF16), right.astype(BF16))
-        at_row = lax.rem(lax.broadcasted_iota(jnp.int32, (tall, wide), 0), strip)
-        at_col = lax.rem(lax.broadcasted_iota(jnp.int32, (tall, wide), 1), strip)
-        mix_v[...] = jnp.where(at_row == at_col, filled, 0.0).astype(BF16)
-
-    def one_strip(s, carry):
-        cells = pl.ds(pl.multiple_of(s * strip, strip), strip)
-        own = field_ref[:, 0, cells, :].reshape(channels * strip, zlen)
-        other = other_ref[:, 0, cells, :].reshape(channels * strip, zlen)
-        local = dot(mix_v[...], jnp.concatenate([own, other], axis=0))
-        waves = ty_ref[my, pl.ds(pl.multiple_of(step * rows + s * strip, strip), strip), :]
-        for o in range(channels):
-            x = dot(waves, g_v[o]) + local[o * strip : (o + 1) * strip]
-            x = x + shift_ref[0, mz * channels + o]
-            inner = x * (0.7978845608028654 + 0.035677408136300125 * (x * x))
-            half = 0.5 * x
-            out_ref[o, 0, cells, :] = (half + half * jnp.tanh(inner)).astype(BF16)
-        return carry
-
-    lax.fori_loop(0, rows // strip, one_strip, 0)
-
-
-def cells(field, other, lines, pointwise, shift, count_y):
-    channels, planes, rows, zlen = field.shape
+    channels, rows, zlen = local_v.shape
+    part = min(rows, 256)
+
+    small = [
+        pltpu.make_async_copy(source, target, small_sem.at[index])
+        for index, (source, target) in enumerate(
+            [(m_hbm, m_v), (gz_hbm, gz_v), (ty_hbm.at[my], ty_v)]
+        )
+    ]
+    loads = [
+        pltpu.make_async_copy(local_hbm.at[o], local_v.at[o], local_sem.at[o])
+        for o in range(channels)
+    ]
+    stores = [
+        pltpu.make_async_copy(out_v.at[o], out_hbm.at[o, 0], out_sem.at[o])
+        for o in range(channels)
+    ]
+    for copy in small + loads:
+        copy.start()
+    for copy in small:
+        copy.wait()
+
+    lines = jnp.transpose(m_v[...]).astype(BF16)
+    both = dot(lines, gz_v[...]) * (0.5 * inverse_scale)
+    both = both.reshape(channels, 2, KY, 2 * zlen)
+    re, im = both[:, 0], both[:, 1]
+    g_v[:, :KY, :] = (re[..., :zlen] + im[..., zlen:]).astype(BF16)
+    g_v[:, KY:, :] = (re[..., zlen:] - im[..., :zlen]).astype(BF16)
+
+    for o in range(channels):
+        offset = 0.5 * shift_ref[0, mz * channels + o]
+        loads[o].wait()
+        for start in range(0, rows, part):
+            cells = pl.ds(start, part)
+            half = dot(ty_v[cells, :], g_v[o]) + local_v[o, cells, :].astype(F32) + offset
+            inner = half * (1.5957691216057308 + 0.285419267290401 * (half * half))
+            out_v[o, cells, :] = (half + half * jnp.tanh(inner)).astype(BF16)
+        stores[o].start()
+    for copy in stores:
+        copy.wait()
+
+
+def cells(local, lines, shift, shape, count_y):
+    channels, planes, rows, zlen = shape
     inverse_scale = 1.0 / math.sqrt(2 * KX * KY * KZ)
-    tile = min(rows, 64)
-    strip = 16
-    slab = pl.BlockSpec((channels, 1, tile, zlen), lambda i: (0, 0, i, 0))
-    vmem = pl.BlockSpec(memory_space=pltpu.VMEM)
+    hbm = pl.BlockSpec(memory_space=pl.ANY)
     smem = pl.BlockSpec(memory_space=pltpu.SMEM)
+    gz_table = inverse_z_table(zlen)
+    ty_table = inverse_y_table(count_y, rows)
+    dma = pltpu.SemaphoreType.DMA
     return pl.pallas_call(
-        functools.partial(cells_kernel, inverse_scale, strip),
-        grid=(rows // tile,),
-        out_shape=jax.ShapeDtypeStruct(field.shape, BF16),
-        in_specs=[slab, slab, vmem, vmem, vmem, vmem, smem],
-        out_specs=slab,
+        functools.partial(cells_kernel, inverse_scale),
+        out_shape=jax.ShapeDtypeStruct(shape, BF16),
+        in_specs=[hbm, hbm, hbm, hbm, smem],
+        out_specs=hbm,
         scratch_shapes=[
+            pltpu.VMEM((channels, rows, zlen), BF16),
+            pltpu.VMEM(lines.shape, F32),
+            pltpu.VMEM(gz_table.shape, BF16),
+            pltpu.VMEM(ty_table.shape[1:], BF16),
+            pltpu.VMEM((channels, rows, zlen), BF16),
             pltpu.VMEM((channels, 2 * KY, zlen), BF16),
-            pltpu.VMEM((channels * strip, CH * strip), BF16),
+            dma((3,)),
+            dma((channels,)),
+            dma((channels,)),
         ],
-        compiler_params=pltpu.CompilerParams(vmem_limit_bytes=40 * 1024 * 1024),
+        compiler_params=pltpu.CompilerParams(vmem_limit_bytes=VMEM_BYTES),
         name="cells",
     )(
-        field,
-        other,
+        local,
         lines,
-        inverse_z_table(zlen),
-        inverse_y_table(count_y, rows),
-        pointwise,
+        jnp.asarray(gz_table),
+        jnp.asarray(ty_table),
         shift,
     )
 
@@ -464,10 +560,10 @@
     count_x = lax.axis_size("gx")
     count_y = lax.axis_size("gy")
     for layer in range(spectral.shape[0]):
-        other, lines = modes(field, spectral[layer : layer + 1], count_x, count_y)
-        field = cells(
-            field, other, lines, pointwise[layer : layer + 1], shift[layer : layer + 1], count_y
-        )
+        local, lines = modes(
+            field, spectral[layer : layer + 1], pointwise[layer : layer + 1], count_x, count_y
+        )
+        field = cells(local, lines, shift[layer : layer + 1], field.shape, count_y)
     return field
 
 

time: 45.7 us -> 31.1 us (0.68)
  local copies, waits for them, and re-layouts: 9.1 us -> 0 us
  Pallas kernels: 36.2 us -> 31 us
    unnamed x24 -> x0, local copies, waits for them, and re-layouts: 9.1 us -> none
    pallas_call x1, Pallas kernels: 12.1 us -> 8.26 us  [cells(): pl.pallas_call(functools.partial(cells_kernel, inverse_scale), out_shape=...]
    pallas_call x1, Pallas kernels: 24.1 us -> 22.7 us  [modes(): pl.pallas_call(functools.partial(modes_kernel, count_x, count_y, forward_...]
where the time goes in v2:
time: 31.1 us; the launch traced here: 31 us
  Pallas kernels  31 us (100%)
    pallas_call x1, Pallas kernels, modes(): pl.pallas_call(functools.partial(modes_kernel, count_x, count_y, forward_...  22.7 us
    pallas_call x1, Pallas kernels, cells(): pl.pallas_call(functools.partial(cells_kernel, inverse_scale), out_shape=...  8.26 us

profile of v2, /device:TPU:0, one launch (start us, length us, event | category | flops | bytes accessed | tf_op | source)
XLA Modules:
  0.0 31.0 jit_solution(4554500231828148802)
XLA Ops:
  0.0 22.7 %modes.1 = (bf16[8,512,512]{2,1,0:T(8,128)(2,1)}, f32[32,512]{1,0:T(8,128)}) custom-call(bf16[8,1,512,512]{3,2,1,0:T(8,128)(2,1)} %field_hbm.1, bf16[1,8,16,16,512]{4,3,2,1,0:T(8,128)(2,1)} %weights_hbm.1, bf16[5760,128]{1,0:T(8,128)(2,1)} %constant.6.clone.table_hbm, bf16[1,16,16]{2,1,0:T(8,128)(2,1)} %point_hbm.1), custom_call_target="tpu_custom_call" | custom-call | tf_op jit(solution)/shard_map/modes/pallas_call | solution.py:426
  22.7 8.3 %cells.1 = bf16[8,1,512,512]{3,2,1,0:T(8,128)(2,1)} custom-call(bf16[8,512,512]{2,1,0:T(8,128)(2,1)} %get-tuple-element.7.local_hbm, f32[32,512]{1,0:T(8,128)} %get-tuple-element.8.m_hbm, bf16[32,1024]{1,0:T(8,128)(2,1)} %constant.7.clone.gz_hbm, bf16[2,512,64]{2,1,0:T(8,128)(2,1)} %constant.8.clone.ty_hbm, f32[1,16]{1,0:T(1,128)} %shift_ref.1), custom_call_target="tpu_custom_call" | custom-call | tf_op jit(solution)/shard_map/cells/pallas_call | solution.py:532

commit v3 on v2

--- a/solution.py
+++ b/solution.py
@@ -14,7 +14,7 @@
 KY = 32
 KZ = 32
 LANES = 128
-VMEM_BYTES = 60 * 1024 * 1024
+VMEM_BYTES = 53 * 1024 * 1024
 MESH = pl.DeviceIdType.MESH
 BF16 = jnp.bfloat16
 F32 = jnp.float32
@@ -186,12 +186,8 @@
     small.append(pltpu.make_async_copy(point_hbm.at[0], point_v, table_sem.at[len(small)]))
     fz_copy, ty_copy, *table_copies = small
     fz_copy.start()
-    for copy in in_copies:
-        copy.start()
-    ty_copy.start()
-    for copy in table_copies:
-        copy.start()
-    weight_copy.start()
+    for copy in in_copies[:3]:
+        copy.start()
 
     peers = [(0, dy, 0) for dy in range(1, count_y)]
     gather = [(dx, 0, dz) for dx in range(count_x) for dz in range(2) if (dx, dz) != (0, 0)]
@@ -217,11 +213,11 @@
         for c in range(channels)
     ]
     for c in range(channels):
-        if c == channels // 2:
-            pl.semaphore_wait(barrier, len(everyone))
-            for copy in field_sends:
-                copy.start()
         in_copies[c].wait()
+        if c + 3 < channels:
+            in_copies[c + 3].start()
+        elif c + 3 == channels:
+            ty_copy.start()
         zhat = rows_cols_dot(fz, field_v[c])
         for d in range(count_y):
             for p in range(2):
@@ -229,6 +225,9 @@
                 zs[d, p, c // 4, pl.ds((c % 4) * kz_each, kz_each), :] = zhat[
                     row : row + kz_each, :
                 ]
+    for copy in table_copies:
+        copy.start()
+    weight_copy.start()
     ty_copy.wait()
     for d in range(count_y):
         total = None
@@ -249,7 +248,10 @@
         )
 
     a_copies = [a_copy(dy) for dy in range(1, count_y)]
+    pl.semaphore_wait(barrier, len(everyone))
     for copy in a_copies:
+        copy.start()
+    for copy in field_sends:
         copy.start()
     total = sa[my].astype(F32)
     for index, copy in enumerate(a_copies):
@@ -322,7 +324,7 @@
             p2_v[k, pl.ds(kz, 1), :] = jnp.sum(weight * second, axis=0, keepdims=True)
         return carry
 
-    lax.fori_loop(0, kz_each, mix, 0)
+    lax.fori_loop(0, kz_each, mix, 0, unroll=4)
 
     width = weights_v.shape[-1]
     lane = lax.broadcasted_iota(jnp.int32, (kz_each, width), 1)
@@ -492,11 +494,17 @@
         pltpu.make_async_copy(local_hbm.at[o], local_v.at[o], local_sem.at[o])
         for o in range(channels)
     ]
+    parts = rows // part
     stores = [
-        pltpu.make_async_copy(out_v.at[o], out_hbm.at[o, 0], out_sem.at[o])
+        pltpu.make_async_copy(
+            out_v.at[o, pl.ds(i * part, part), :],
+            out_hbm.at[o, 0, pl.ds(i * part, part), :],
+            out_sem.at[o * parts + i],
+        )
         for o in range(channels)
-    ]
-    for copy in small + loads:
+        for i in range(parts)
+    ]
+    for copy in small + loads[:2]:
         copy.start()
     for copy in small:
         copy.wait()
@@ -511,12 +519,14 @@
     for o in range(channels):
         offset = 0.5 * shift_ref[0, mz * channels + o]
         loads[o].wait()
+        if o + 2 < channels:
+            loads[o + 2].start()
         for start in range(0, rows, part):
             cells = pl.ds(start, part)
             half = dot(ty_v[cells, :], g_v[o]) + local_v[o, cells, :].astype(F32) + offset
             inner = half * (1.5957691216057308 + 0.285419267290401 * (half * half))
             out_v[o, cells, :] = (half + half * jnp.tanh(inner)).astype(BF16)
-        stores[o].start()
+            stores[o * parts + start // part].start()
     for copy in stores:
         copy.wait()
 
@@ -543,7 +553,7 @@
             pltpu.VMEM((channels, 2 * KY, zlen), BF16),
             dma((3,)),
             dma((channels,)),
-            dma((channels,)),
+            dma((channels * (rows // min(rows, 256)),)),
         ],
         compiler_params=pltpu.CompilerParams(vmem_limit_bytes=VMEM_BYTES),
         name="cells",

time: 31.1 us -> 29.9 us (0.961)
  Pallas kernels: 31 us -> 28.8 us
  local copies, waits for them, and re-layouts: 0 us -> 0.74 us
    pallas_call x1, Pallas kernels: 22.7 us -> 21.6 us  [modes(): pl.pallas_call(functools.partial(modes_kernel, count_x, count_y, forward_...]
    pallas_call x1, Pallas kernels: 8.26 us -> 7.22 us  [cells(): pl.pallas_call(functools.partial(cells_kernel, inverse_scale), out_shape=...]
    unnamed x0 -> x8, local copies, waits for them, and re-layouts: none -> 0.74 us
where the time goes in v3:
time: 29.9 us; the launch traced here: 29.6 us
  Pallas kernels  28.8 us (96%)
  local copies, waits for them, and re-layouts  0.74 us (2%)
    pallas_call x1, Pallas kernels, modes(): pl.pallas_call(functools.partial(modes_kernel, count_x, count_y, forward_...  21.6 us
    pallas_call x1, Pallas kernels, cells(): pl.pallas_call(functools.partial(cells_kernel, inverse_scale), out_shape=...  7.22 us
    unnamed x8, local copies, waits for them, and re-layouts  0.74 us

profile of v3, /device:TPU:0, one launch (start us, length us, event | category | flops | bytes accessed | tf_op | source)
XLA Modules:
  0.0 29.6 jit_solution(5021380923046208235)
XLA Ops:
  0.0 0.0 copy-start
  0.0 0.0 copy-start.1
  0.0 0.0 copy-start.2
  0.0 0.7 %copy-done.2 = bf16[1,16,16]{2,1,0:T(8,128)(2,1)S(1)} copy-done((bf16[1,16,16]{2,1,0:T(8,128)(2,1)S(1)}, bf16[1,16,16]{2,1,0:T(8,128)(2,1)}, u32[]{:S(2)}) %copy-start.2) | copy-done | bytes 536
  0.7 0.0 copy-start.3
  0.7 21.6 %modes.1 = (bf16[8,512,512]{2,1,0:T(8,128)(2,1)}, f32[32,512]{1,0:T(8,128)S(1)}) custom-call(bf16[8,1,512,512]{3,2,1,0:T(8,128)(2,1)} %field_hbm.1, bf16[1,8,16,16,512]{4,3,2,1,0:T(8,128)(2,1)} %weights_hbm.1, bf16[5760,128]{1,0:T(8,128)(2,1)} %constant.6.clone.table_hbm, bf16[1,16,16]{2,1,0:T(8,128)(2,1)S(1)} %copy-done.2), custom_call_target="tpu_custom_call" | custom-call | tf_op jit(solution)/shard_map/modes/pallas_call | solution.py:428
  22.4 0.0 copy-done
  22.4 0.0 copy-done.1
  22.4 0.0 copy-done.3
  22.4 7.2 %cells.1 = bf16[8,1,512,512]{3,2,1,0:T(8,128)(2,1)} custom-call(bf16[8,512,512]{2,1,0:T(8,128)(2,1)} %get-tuple-element.7.local_hbm, f32[32,512]{1,0:T(8,128)S(1)} %get-tuple-element.8.m_hbm, bf16[32,1024]{1,0:T(8,128)(2,1)S(1)} %copy-done.1, bf16[2,512,64]{2,1,0:T(8,128)(2,1)S(1)} %copy-done, f32[1,16]{1,0:T(1,128)S(1)} %copy-done.3), custom_call_target="tpu_custom_call" | custom-call | tf_op jit(solution)/shard_map/cells/pallas_call | solution.py:542
Async XLA Ops:
  0.0 22.4 %copy-start = (bf16[2,512,64]{2,1,0:T(8,128)(2,1)S(1)}, bf16[2,512,64]{2,1,0:T(8,128)(2,1)}, u32[]{:S(2)}) copy-start(bf16[2,512,64]{2,1,0:T(8,128)(2,1)} %constant.8.clone.ty_hbm) | copy-start | bytes 393220
  0.0 22.4 %copy-start.1 = (bf16[32,1024]{1,0:T(8,128)(2,1)S(1)}, bf16[32,1024]{1,0:T(8,128)(2,1)}, u32[]{:S(2)}) copy-start(bf16[32,1024]{1,0:T(8,128)(2,1)} %constant.7.clone.gz_hbm) | copy-start | bytes 196612
  0.0 0.7 %copy-start.2 = (bf16[1,16,16]{2,1,0:T(8,128)(2,1)S(1)}, bf16[1,16,16]{2,1,0:T(8,128)(2,1)}, u32[]{:S(2)}) copy-start(bf16[1,16,16]{2,1,0:T(8,128)(2,1)} %point_hbm.1) | copy-start | bytes 1540
  0.7 21.6 %copy-start.3 = (f32[1,16]{1,0:T(1,128)S(1)}, f32[1,16]{1,0:T(1,128)}, u32[]{:S(2)}) copy-start(f32[1,16]{1,0:T(1,128)} %shift_ref.1) | copy-start | bytes 196
